TPU v7x, 256 devices: a whole 4x4x8 slice. The times are simulated.
256 devices in a mesh: design: 16 (over z_hi, y, core), offset: 16 (over z_lo, x).
Axes of the slice: x: 4, y: 4, z: 8 (z_hi: 2, z_lo: 4; z = z_hi * 4 + z_lo), core: 2. Of those that a mesh axis runs over, the one named last changes fastest.
Arguments:
- snapshots: bfloat16 [4096, 256, 1024], P('design', 'offset'), may hold values from -6 to 6
- start_basis: bfloat16 [256, 64, 1024], P('offset'), may hold values from -0.01171875 to 0.01171875
- start_moments: float32 [64, 64], replicated, may hold values from -6 to 6
- station_power: int32 [64], replicated, may hold values from 0 to 4
- girth_power: int32 [64], replicated, may hold values from 0 to 4
- slab_id: int32 [4096], P('design'), may hold values from 0 to 7
- slab_scale: float32 [8], replicated, may hold values from 0.5 to 2
Outputs:
- basis: bfloat16 [256, 64, 1024], P('offset')
- basis_moments: float32 [64, 64], replicated
- moments: float32 [4096, 64], P('design')
All inputs are finite; a program needn't handle non-finite values.
Results may differ from a plain program's by a relative error of at most 0.012.
Values may be sent and summed in bfloat16 or wider, within the bound.
A program may use at most 64 MiB of HBM per device.

v0:
```python
import jax
import jax.numpy as jnp
from jax import lax
from jax.sharding import PartitionSpec as P

STATIONS = 256
GIRTH = 1024
SLABS = 8


HIGH = lax.Precision.HIGHEST


def power_table(coord, powers):
    table = jnp.stack([coord**j for j in range(5)], 0)
    picks = (powers[None, :] == jnp.arange(5, dtype=jnp.int32)[:, None]).astype(jnp.float32)
    return jnp.einsum("jp,jm->pm", table, picks, precision=HIGH)


def finish_gram(gram_part, images_moments):
    gram = (gram_part + jnp.dot(images_moments.T, images_moments, precision=HIGH)) / (
        STATIONS * GIRTH
    )
    lower = jnp.linalg.cholesky(gram)
    return lax.linalg.triangular_solve(
        lower, jnp.eye(gram.shape[0], dtype=jnp.float32), left_side=True, lower=True
    )


def body(snapshots, start_basis, start_moments, station_power, girth_power, slab_id, slab_scale):
    local_rows = snapshots.shape[1]
    first_row = lax.axis_index("offset") * local_rows
    t_coord = (first_row + jnp.arange(local_rows, dtype=jnp.int32)).astype(jnp.float32)
    t_coord = (t_coord + 0.5) / STATIONS
    u_coord = 2.0 * (jnp.arange(GIRTH, dtype=jnp.float32) + 0.5) / GIRTH - 1.0
    station_weight = power_table(t_coord, station_power)
    girth_weight = power_table(u_coord, girth_power).astype(jnp.bfloat16)
    inner = jnp.einsum("dsg,gm->dsm", snapshots, girth_weight, preferred_element_type=jnp.float32)
    raw_part = jnp.sum(inner * station_weight[None], 1)
    proj_part = jnp.einsum(
        "dsg,skg->dk", snapshots, start_basis, preferred_element_type=jnp.float32
    )
    picks = (slab_id[:, None] == jnp.arange(SLABS, dtype=jnp.int32)[None, :]).astype(jnp.float32)
    scale = jnp.sum(picks * slab_scale[None, :], 1) / jnp.sqrt(jnp.float32(STATIONS * GIRTH))
    moments = lax.psum(raw_part, "offset") * scale[:, None]
    coords = lax.psum(proj_part, "offset") + jnp.dot(moments, start_moments, precision=HIGH)
    coords_low = coords.astype(jnp.bfloat16)
    moment_term = jnp.dot(moments.T, coords_low.astype(jnp.float32), precision=HIGH)
    image_term = jnp.einsum(
        "dk,dsg->skg", coords_low, snapshots, preferred_element_type=jnp.float32
    )
    images, images_moments = lax.psum((image_term, moment_term), "design")
    gram_part = lax.psum(jnp.einsum("skg,slg->kl", images, images, precision=HIGH), "offset")
    inverse = finish_gram(gram_part, images_moments)
    basis = jnp.einsum("kl,slg->skg", inverse, images, precision=HIGH).astype(jnp.bfloat16)
    basis_moments = jnp.dot(images_moments, inverse.T, precision=HIGH)
    return (basis, basis_moments, moments)


def solution(mesh):
    in_specs = (
        P("design", "offset", None),
        P("offset", None, None),
        P(),
        P(),
        P(),
        P("design"),
        P(),
    )
    out_specs = (P("offset", None, None), P(), P("design", None))
    return jax.shard_map(body, mesh=mesh, in_specs=in_specs, out_specs=out_specs, check_vma=False)
```

profile of v0, /device:TPU:0, one launch (start us, length us, event | category | flops | bytes accessed | tf_op | source)
XLA Modules:
  0.0 514.0 jit_solution(15904246215262457087)
XLA Ops:
  7.2 0.0 copy-start
  7.2 0.0 all-reduce.6.cloned.1.call-start
  7.4 1.0 fusion.30
  8.3 0.5 copy-done
  8.8 0.0 copy-start.4
  8.8 13.0 %fusion.19 = f32[256,64]{0,1:T(8,128)} fusion(bf16[16,64,1024]{2,1,0:T(8,128)(2,1)S(1)} %copy-done, bf16[256,16,1024]{2,1,0:T(8,128)(2,1)} %param.7), kind=kOutput, calls=%fused_computation.13 | convolution fusion | flops 536870912 | bytes 10551296 | tf_op jit(solution)/shard_map/dsg,skg->dk/dot_general | solution.py:40
  21.9 0.0 copy-done.4
  21.9 0.3 fusion.18
  22.2 0.0 copy-start.3
  22.2 0.0 copy-start.5
  22.2 0.0 copy-start.2
  22.2 9.1 %fusion.15 = f32[256,64]{0,1:T(8,128)} fusion(bf16[1024,64,1]{0,1,2:T(8,128)(2,1)S(1)} %fusion.18, bf16[256,16,1024]{2,1,0:T(8,128)(2,1)} %param.7, f32[16,64]{1,0:T(8,128)S(1)} %fusion.30), kind=kOutput, calls=%fused_computation.10 | convolution fusion | flops 537378816 | bytes 8589312 | tf_op jit(solution)/shard_map/dsg,gm->dsm/dot_general | solution.py:38
  31.4 0.0 all-reduce.6.cloned.1.call-update
  31.4 0.0 all-reduce.4.cloned.1.call-start
  31.4 0.0 copy-done.3
  31.4 0.0 copy-done.5
  31.5 0.1 select_reduce_fusion.1
  31.5 160.4 %all-reduce.6.cloned.1.call-done = (f32[256,64]{0,1:T(8,128)}, f32[256,64]{0,1:T(8,128)}) async-done(((f32[256,64]{0,1:T(8,128)}, f32[256,64]{0,1:T(8,128)}), (f32[256,64]{0,1:T(8,128)}, f32[256,64]{0,1:T(8,128)})) %all-reduce.6.cloned.1.call-update) | async-done | bytes 131088 | tf_op jit(solution)/shard_map/psum | solution.py:46
  192.0 0.8 broadcast_multiply_fusion
  192.8 0.0 copy-start.1
  192.8 0.0 copy-done.2
  192.8 1.1 fusion.22
  194.0 14.7 %fusion.6 = f32[16,64,1024]{2,1,0:T(8,128)} fusion(bf16[256,16,1024]{2,1,0:T(8,128)(2,1)} %param.7, bf16[256,64]{0,1:T(8,128)(2,1)S(1)} %fusion.22), kind=kOutput, calls=%fused_computation.6 | convolution fusion | flops 536870912 | bytes 12615680 | tf_op jit(solution)/shard_map/dk,dsg->skg/dot_general | solution.py:49
  208.7 0.0 all-reduce.4.cloned.1.call-update
  208.7 0.0 copy-done.1
  208.7 0.2 fusion.37
  208.9 86.2 %psum.39 = f32[64,64]{1,0:T(8,128)S(1)} all-reduce(f32[64,64]{1,0:T(8,128)S(1)} %fusion.37), channel_id=1, replica_groups=mesh['design'=16,'offset'=16] {'design'}, use_global_device_ids=true, to_apply=%region_6.0 | all-reduce | flops 4096 | bytes 32768 | tf_op jit(solution)/shard_map/psum | solution.py:52
  295.1 108.7 %all-reduce.4.cloned.1.call-done = f32[16,64,1024]{2,1,0:T(8,128)} async-done(((f32[16,64,1024]{2,1,0:T(8,128)}), f32[16,64,1024]{2,1,0:T(8,128)}) %all-reduce.4.cloned.1.call-update) | async-done | bytes 4194320 | tf_op jit(solution)/shard_map/psum | solution.py:52
  403.8 6.9 %convolution_bitcast_fusion = f32[64,64]{0,1:T(8,128)S(1)} fusion(f32[16,64,1024]{2,1,0:T(8,128)} %all-reduce.4.cloned.1.call-done), kind=kOutput, calls=%fused_computation.18 | convolution fusion | flops 805306368 | bytes 4210688 | tf_op jit(solution)/shard_map/skg,slg->kl/dot_general | solution.py:53
  410.7 75.5 %psum.38 = f32[64,64]{0,1:T(8,128)S(1)} all-reduce(f32[64,64]{0,1:T(8,128)S(1)} %convolution_bitcast_fusion), channel_id=1, replica_groups=mesh['design'=16,'offset'=16] {'offset'}, use_global_device_ids=true, to_apply=%region_5.0 | all-reduce | flops 4096 | bytes 32768 | tf_op jit(solution)/shard_map/psum | solution.py:53
  486.2 0.2 fusion.23
  486.5 0.1 copy.21
  486.6 5.8 %cholesky.17 = f32[64,64]{1,0:T(8,128)S(1)} custom-call(f32[64,64]{1,0:T(8,128)S(1)} %fusion.28), custom_call_target="Cholesky" | custom-call | tf_op jit(solution)/shard_map/jit(cholesky)/cholesky | solution.py:24
  492.5 0.6 compare_reduce_fusion
  493.1 0.7 fusion.24
  493.8 4.9 custom-call.6
  498.7 0.2 fusion.26
  498.9 0.8 fusion.38
  499.7 7.5 %convert_bitcast_fusion = bf16[16,64,1024]{2,1,0:T(8,128)(2,1)} fusion(f32[16,64,1024]{2,1,0:T(8,128)} %all-reduce.4.cloned.1.call-done, f32[64,64]{1,0:T(8,128)S(1)} %fusion.26), kind=kOutput, calls=%fused_computation.7 | convolution fusion | flops 806354944 | bytes 6307840 | tf_op jit(solution)/shard_map/kl,slg->skg/dot_general | solution.py:55
  (11 shorter events, 0.2 us)
Async XLA Ops:
  7.2 1.6 copy-start
  7.2 184.8 %all-reduce.6.cloned.1.call-start = ((), (), s32[]{:S(2)}) async-start(), calls=%async_computation.1 | async-start | bytes 262144 | tf_op jit(solution)/shard_map/psum | solution.py:46
  8.8 13.1 %copy-start.4 = (s32[64]{0:T(128)S(1)}, s32[64]{0:T(128)}, u32[]{:S(2)}) copy-start(s32[64]{0:T(128)} %param.11) | copy-start | bytes 772
  22.2 9.2 %copy-start.3 = (s32[256]{0:T(256)S(1)}, s32[256]{0:T(256)}, u32[]{:S(2)}) copy-start(s32[256]{0:T(256)} %param.12) | copy-start | bytes 3076
  22.2 9.2 %copy-start.5 = (f32[8]{0:T(128)S(1)}, f32[8]{0:T(128)}, u32[]{:S(2)}) copy-start(f32[8]{0:T(128)} %param.13) | copy-start | bytes 100
  22.2 170.6 %copy-start.2 = (f32[64,64]{1,0:T(8,128)S(1)}, f32[64,64]{1,0:T(8,128)}, u32[]{:S(2)}) copy-start(f32[64,64]{1,0:T(8,128)} %param.9) | copy-start | bytes 49156
  31.4 372.4 %all-reduce.4.cloned.1.call-start = ((), (), s32[]{:S(2)}) async-start(), calls=%async_computation | async-start | bytes 8388608 | tf_op jit(solution)/shard_map/psum | solution.py:52
  192.8 15.8 %copy-start.1 = (f32[256,64]{0,1:T(8,128)}, f32[256,64]{0,1:T(8,128)S(1)}, u32[]{:S(2)}) copy-start(f32[256,64]{0,1:T(8,128)S(1)} %broadcast_multiply_fusion) | copy-start | bytes 196612
Sparse Core Ops, SparseCore 0:
  31.5 160.4 all-reduce.5
  208.8 194.9 all-reduce.3
where the time goes:
time: 514 us
  waiting for transfers between devices  269 us (52%)
  blocking collectives  162 us (32%)
  matrix products  55.1 us (11%)
  between operations  14.2 us (3%)
  other arithmetic  13.1 us (3%)
    psum x1, waiting for transfers between devices, body(): lax.psum(proj_part, 'offset')  160 us
    psum x1, waiting for transfers between devices, body(): images, images_moments = lax.psum((image_term, moment_term), 'design')  109 us
    psum x1, blocking collectives, body(): images, images_moments = lax.psum((image_term, moment_term), 'design')  86.2 us
    psum x1, blocking collectives, body(): lax.psum(jnp.einsum('skg,slg->kl', images, images, precision=HIGH), 'offs...  75.5 us
    dot_general x1, matrix products, body(): jnp.einsum('dk,dsg->skg', coords_low, snapshots, preferred_element_type=j...  14.7 us
    dot_general x1, matrix products, body(): jnp.einsum('dsg,skg->dk', snapshots, start_basis, preferred_element_type=...  13 us
  transfers between devices with their start and end apart: 2, of which 2 were waited for; matrix products, arithmetic and copies ran while one was open for 0% of the time, Pallas kernels for 0%

commit v1 on v0

v1 whole, which is shorter than its diff:
```python
import jax
import jax.numpy as jnp
from jax import lax
from jax.experimental import pallas as pl
from jax.experimental.pallas import tpu as pltpu
from jax.sharding import PartitionSpec as P

STATIONS = 256
GIRTH = 1024
SLABS = 8
K = 64
ROWS = 16
DESIGNS = 256
PARTS = 4
WIDE = GIRTH // PARTS

HIGH = lax.Precision.HIGHEST
MESH = pl.DeviceIdType.MESH
F32 = jnp.float32
LOW = jnp.bfloat16


def iota(shape, axis):
    return lax.broadcasted_iota(jnp.int32, shape, axis)


def column(row, lanes):
    n = row.shape[1]
    tall = jnp.where(iota((8, n), 0) == 0, jnp.broadcast_to(row, (8, n)), 0.0)
    return lax.dot_general(
        tall, jnp.ones((8, lanes), F32), (((0,), (0,)), ((), ())),
        precision=HIGH, preferred_element_type=F32,
    )


def power_of(value, powers):
    square = value * value
    out = jnp.where(powers == 0, 1.0, jnp.where(powers == 1, value, square))
    out = jnp.where(powers == 3, square * value, out)
    return jnp.where(powers == 4, square * square, out)


def inverse_factor(matrix):
    eye = (iota((K, K), 0) == iota((K, K), 1)).astype(F32)
    both = jnp.concatenate([matrix, eye], axis=1)
    blocks = [both[8 * b : 8 * b + 8] for b in range(K // 8)]
    sub = iota((8, 1), 0)
    for j in range(K):
        b, r = j // 8, j % 8
        row = blocks[b][r : r + 1, :]
        row = row / row[:, j : j + 1]
        for i in range(b, K // 8):
            col = blocks[i][:, j : j + 1]
            if i == b:
                if r == 7:
                    continue
                col = jnp.where(sub > r, col, 0.0)
            blocks[i] = blocks[i] - col * row
    out = []
    for b in range(K // 8):
        diag = jnp.sum(
            jnp.where(iota((8, 2 * K), 1) == iota((8, 2 * K), 0) + 8 * b, blocks[b], 0.0),
            axis=1, keepdims=True,
        )
        out.append(blocks[b][:, K:] * lax.rsqrt(diag))
    return jnp.concatenate(out, axis=0)


def fold(square):
    return jnp.concatenate([square[: K // 2], square[K // 2 :]], axis=1)


def unfold(folded):
    return jnp.concatenate([folded[:, :K], folded[:, K:]], axis=0)


def kernel(
    snap_hbm, start_hbm, moments_ref, spow_ref, gpow_ref, slab_ref, slab_scale,
    basis_hbm, basis_moments_ref, moments_out,
    raw, turned, weights, acc, scale_ref, parts_ref, coords_ref, girth_ref,
    core_out, core_in, mine, y_out, y_in, z_out, z_in, full, result,
    im_core, im_y, im_z, gram_1, gram_2, gram_3, gram_total,
    load_sem, part_s, part_r, coord_s, coord_r, core_s, core_r, y_s, y_r, z_s, z_r,
    g_s, g_r, f_s, f_r, im_s, im_r, gr_s, gr_r, out_sem,
):
    de, of = lax.axis_index("design"), lax.axis_index("offset")
    c, y, zh = lax.rem(de, 2), lax.rem(de // 2, 4), de // 8
    zl, x = of // 4, lax.rem(of, 4)

    def at(zh_, y_, c_):
        return ((zh_ * 4 + y_) * 2 + c_, of)

    sibling = at(zh, y, 1 - c)
    beyond = at(1 - zh, y, c)

    def along_y(r):
        return at(zh, lax.rem(y + r, 4), c)

    def copy(src, dst, s_sem, r_sem, to):
        return pltpu.make_async_remote_copy(
            src_ref=src, dst_ref=dst, send_sem=s_sem, recv_sem=r_sem,
            device_id=to, device_id_type=MESH,
        )

    barrier = pltpu.get_barrier_semaphore()

    @pl.loop(1, 16)
    def _(r):
        pl.semaphore_signal(barrier, inc=1, device_id=(lax.rem(de + r, 16), of), device_id_type=MESH)
        pl.semaphore_signal(barrier, inc=1, device_id=(de, lax.rem(of + r, 16)), device_id_type=MESH)

    loads = []
    for q in range(PARTS):
        lanes = pl.ds(q * WIDE, WIDE)
        loads.append(pltpu.make_async_copy(snap_hbm.at[:, :, lanes], raw.at[q], load_sem.at[q]))
        loads[-1].start()
        if q == 0:
            start_load = pltpu.make_async_copy(
                start_hbm, weights.at[:, pl.ds(0, K), :], load_sem.at[PARTS]
            )
            start_load.start()

    spow = spow_ref[...]
    gpow = gpow_ref[...]
    u = (2.0 * (iota((K, GIRTH), 1).astype(F32) + 0.5)) / GIRTH - 1.0
    girth_ref[...] = power_of(u, column(gpow.astype(F32), GIRTH).astype(jnp.int32)).astype(LOW)

    @pl.loop(0, ROWS)
    def _(s):
        weights[s, pl.ds(K, K), :] = girth_ref[...]

    slab = slab_ref[...]
    scale = jnp.zeros((1, DESIGNS), F32)
    square = jnp.float32(0.0)
    for j in range(SLABS):
        scale = jnp.where(slab == j, slab_scale[j], scale)
        square = square + slab_scale[j] * slab_scale[j]
    scale = column(scale / 512.0, 2 * K)
    scale_ref[...] = jnp.where(iota((DESIGNS, 2 * K), 1) < K, 1.0, scale)

    lane_power = jnp.concatenate([jnp.zeros((1, K), jnp.int32), spow], axis=1)
    acc[...] = jnp.zeros_like(acc)
    for q in range(PARTS):
        loads[q].wait()

        @pl.loop(0, DESIGNS // 16)
        def _(i):
            d0 = pl.multiple_of(i * 16, 16)
            for g in range(WIDE // 128):
                v = raw[q, pl.ds(d0, 16), :, pl.ds(g * 128, 128)]
                turned[:, pl.ds(d0, 16), pl.ds(q * WIDE + g * 128, 128)] = jnp.swapaxes(v, 0, 1)

        if q == 0:
            start_load.wait()

        @pl.loop(0, ROWS // 4)
        def _(i):
            total = acc[...]
            for j in range(4):
                s = i * 4 + j
                t = ((of * ROWS + s).astype(F32) + 0.5) / STATIONS
                lanes = pl.ds(q * WIDE, WIDE)
                part = lax.dot_general(
                    turned[s, :, lanes], weights[s, :, lanes], (((1,), (1,)), ((), ())),
                    preferred_element_type=F32,
                )
                total = total + part * power_of(t, lane_power)
            acc[...] = total

    pl.semaphore_wait(barrier, 30)

    def row_block(of_):
        return pl.ds(pl.multiple_of(of_ * ROWS, ROWS), ROWS)

    def part_copy(r):
        to = lax.rem(of + r, 16)
        return copy(acc.at[row_block(to)], parts_ref.at[of], part_s.at[r], part_r.at[of], (de, to))

    def part_arrival(r):
        frm = lax.rem(of + r, 16)
        return copy(acc.at[row_block(of)], parts_ref.at[frm], part_s.at[r], part_r.at[frm], (de, frm))

    @pl.loop(1, 16)
    def _(r):
        part_copy(r).start()

    parts_ref[of] = acc[row_block(of), :]

    pc = column(spow.astype(F32), K) + spow.astype(F32)
    qc = column(gpow.astype(F32), K) + gpow.astype(F32)
    even = lax.rem(qc.astype(jnp.int32), 2) == 0
    overlap = jnp.where(even, (square / SLABS) / ((pc + 1.0) * (qc + 1.0)), 0.0)
    start_moments = moments_ref[...]
    model = lax.dot_general(
        start_moments, jnp.dot(overlap, start_moments, precision=HIGH, preferred_element_type=F32),
        (((0,), (0,)), ((), ())), precision=HIGH, preferred_element_type=F32,
    )
    eye = iota((K, K), 0) == iota((K, K), 1)
    model = model + jnp.where(eye, 1.0, 0.0)
    turn = inverse_factor(model)

    @pl.loop(1, 16)
    def _(r):
        part_arrival(r).wait_recv()

    summed = parts_ref[0]
    for j in range(1, 16):
        summed = summed + parts_ref[j]
    summed = summed * scale_ref[row_block(of), :]
    own_moments = summed[:, K:]
    coords = summed[:, :K] + jnp.dot(
        own_moments, start_moments, precision=HIGH, preferred_element_type=F32
    )
    coords = coords.astype(LOW).astype(F32)
    coords = lax.dot_general(
        coords, turn, (((1,), (1,)), ((), ())), precision=HIGH, preferred_element_type=F32
    )
    coords_ref[row_block(of), :] = jnp.concatenate([coords, own_moments], axis=1)

    def coord_copy(r):
        to = lax.rem(of + r, 16)
        return copy(
            coords_ref.at[row_block(of)], coords_ref.at[row_block(of)],
            coord_s.at[r], coord_r.at[of], (de, to),
        )

    def coord_arrival(r):
        frm = lax.rem(of + r, 16)
        return copy(
            coords_ref.at[row_block(frm)], coords_ref.at[row_block(frm)],
            coord_s.at[r], coord_r.at[frm], (de, frm),
        )

    @pl.loop(1, 16)
    def _(r):
        coord_copy(r).start()

    @pl.loop(1, 16)
    def _(r):
        coord_arrival(r).wait_recv()

    coords = coords_ref[:, :K]
    moments = coords_ref[:, K:]
    moments_out[...] = moments
    tall = jnp.transpose(coords_ref[...])[:K].astype(LOW)

    pending = []

    def send(src, dst, s_sem, r_sem, to):
        cp = copy(src, dst, s_sem, r_sem, to)
        cp.start()
        pending.append(cp)
        return cp

    images_moments = lax.dot_general(
        moments, coords, (((0,), (0,)), ((), ())), precision=HIGH, preferred_element_type=F32
    )
    im_core[0] = fold(images_moments)

    def images(q):
        lanes = pl.ds(q * WIDE, WIDE)

        @pl.loop(0, 2)
        def _(i):
            for j in range(4):
                n = i * 4 + j
                core_out[q, n] = jnp.dot(
                    tall, turned[(1 - c) * 8 + n, :, lanes], preferred_element_type=F32
                ).astype(LOW)

        cp = send(core_out.at[q], core_in.at[q], core_s.at[q], core_r.at[q], sibling)

        @pl.loop(0, 2)
        def _(i):
            for j in range(4):
                n = i * 4 + j
                mine[q, n] = jnp.dot(
                    tall, turned[c * 8 + n, :, lanes], preferred_element_type=F32
                )

        return cp

    def to_y(q, cp):
        cp.wait_recv()

        @pl.loop(0, 8)
        def _(n):
            y_out[q, n] = (mine[q, n] + core_in[q, n].astype(F32)).astype(LOW)

        cps = []
        for r in (2, 1, 3):
            pair = pl.ds(2 * lax.rem(y + r, 4), 2)
            cps.append(
                send(y_out.at[q, pair], y_in.at[q, r - 1], y_s.at[q, r - 1], y_r.at[q, r - 1], along_y(r))
            )
        return cps

    def to_z(q, cps):
        for cp in cps:
            cp.wait_recv()
        for h in range(2):
            n = 2 * y + h
            total = mine[q, n] + core_in[q, n].astype(F32)
            for r in range(3):
                total = total + y_in[q, r, h].astype(F32)
            z_out[q, h] = total.astype(LOW)
        return send(z_out.at[q], z_in.at[q], z_s.at[q], z_r.at[q], beyond)

    first = c * 8 + 2 * y

    def gather(q, cp, gram):
        cp.wait_recv()
        for h in range(2):
            image = (z_out[q, h].astype(F32) + z_in[q, h].astype(F32)).astype(LOW)
            full[q, first + h] = image
            gram = gram + lax.dot_general(
                image, image, (((1,), (1,)), ((), ())), preferred_element_type=F32
            )
        pair = full.at[q, pl.ds(first, 2)]
        cps = [
            send(pair, pair, g_s.at[q, r - 1], g_r.at[q, r - 1], along_y(r)) for r in (2, 1, 3)
        ]
        cps.append(send(pair, pair, f_s.at[q, 0], f_r.at[q, 0], sibling))
        return cps, gram

    def hand_on(q, cps):
        for cp, r in zip(cps[:3], (2, 1, 3)):
            cp.wait_recv()
            frm = lax.rem(y + 4 - r, 4)
            pair = full.at[q, pl.ds(c * 8 + 2 * frm, 2)]
            send(pair, pair, f_s.at[q, r], f_r.at[q, r], sibling)

    def exchange(ref, slot, members, sems):
        cps = []
        for r, to in members:
            cps.append(send(ref.at[slot], ref.at[slot], gr_s.at[sems + r], gr_r.at[sems + r], to))
        return cps

    core_im = send(im_core.at[0], im_core.at[1], im_s.at[0], im_r.at[0], sibling)
    core_cp = [None] * PARTS
    y_cp = [None] * PARTS
    z_cp = [None] * PARTS
    g_cp = [None] * PARTS
    core_cp[0] = images(0)
    core_cp[1] = images(1)
    y_cp[0] = to_y(0, core_cp[0])
    core_cp[2] = images(2)
    y_cp[1] = to_y(1, core_cp[1])
    core_im.wait_recv()
    im_y[y] = im_core[0] + im_core[1]
    im_cps = [
        send(im_y.at[y], im_y.at[y], im_s.at[r], im_r.at[r], along_y(r)) for r in (1, 2, 3)
    ]
    core_cp[3] = images(3)
    y_cp[2] = to_y(2, core_cp[2])
    y_cp[3] = to_y(3, core_cp[3])
    for cp in im_cps:
        cp.wait_recv()
    im_z[0] = (im_y[0] + im_y[1]) + (im_y[2] + im_y[3])
    im_cp = send(im_z.at[0], im_z.at[1], im_s.at[4], im_r.at[4], beyond)

    gram = jnp.zeros((K, K), F32)
    z_cp[0] = to_z(0, y_cp[0])
    z_cp[1] = to_z(1, y_cp[1])
    g_cp[0], gram = gather(0, z_cp[0], gram)
    z_cp[2] = to_z(2, y_cp[2])
    g_cp[1], gram = gather(1, z_cp[1], gram)
    z_cp[3] = to_z(3, y_cp[3])
    g_cp[2], gram = gather(2, z_cp[2], gram)
    g_cp[3], gram = gather(3, z_cp[3], gram)

    me = 2 * y + c
    gram_1[me] = fold(gram)
    cps = []
    for r in range(1, 8):
        ry, rc = r // 2, r % 2
        to = at(zh, lax.rem(y + ry, 4), lax.rem(c + rc, 2))
        cps.append((r, to))
    cps = exchange(gram_1, me, cps, 0)
    im_cp.wait_recv()
    images_moments = unfold(im_z[0] + im_z[1])
    hand_on(0, g_cp[0])
    for cp in cps:
        cp.wait_recv()
    total = gram_1[0]
    for j in range(1, 8):
        total = total + gram_1[j]
    gram_2[x] = total
    cps = exchange(gram_2, x, [(r, (de, zl * 4 + lax.rem(x + r, 4))) for r in (1, 2, 3)], 7)
    for cp in cps:
        cp.wait_recv()
    gram_3[zl] = (gram_2[0] + gram_2[1]) + (gram_2[2] + gram_2[3])
    cps = exchange(gram_3, zl, [(r, (de, lax.rem(zl + r, 4) * 4 + x)) for r in (1, 2, 3)], 10)
    hand_on(1, g_cp[1])
    for cp in cps:
        cp.wait_recv()
    gram = unfold((gram_3[0] + gram_3[1]) + (gram_3[2] + gram_3[3]))
    gram = gram + lax.dot_general(
        images_moments, images_moments, (((0,), (0,)), ((), ())),
        precision=HIGH, preferred_element_type=F32,
    )
    inverse = inverse_factor(gram / (STATIONS * GIRTH))
    hand_on(2, g_cp[2])
    hand_on(3, g_cp[3])
    basis_moments_ref[...] = lax.dot_general(
        images_moments, inverse, (((1,), (1,)), ((), ())),
        precision=HIGH, preferred_element_type=F32,
    )
    high = inverse.astype(LOW)
    pieces = jnp.concatenate([high, (inverse - high.astype(F32)).astype(LOW)], axis=0)

    for q in range(PARTS):
        for r in range(4):
            frm = lax.rem(y + 4 - r, 4)
            pair = full.at[q, pl.ds((1 - c) * 8 + 2 * frm, 2)]
            copy(pair, pair, f_s.at[q, r], f_r.at[q, r], sibling).wait_recv()

    outs = []
    for i in range(4):
        for j in range(4):
            s = i * 4 + j
            for q in range(PARTS):
                out = jnp.dot(pieces, full[q, s], preferred_element_type=F32)
                result[s, :, pl.ds(q * WIDE, WIDE)] = (out[:K] + out[K:]).astype(LOW)
        block = pl.ds(i * 4, 4)
        outs.append(pltpu.make_async_copy(result.at[block], basis_hbm.at[block], out_sem.at[i]))
        outs[-1].start()

    @pl.loop(1, 16)
    def _(r):
        part_copy(r).wait_send()
        coord_copy(r).wait_send()

    for cp in pending:
        cp.wait_send()
    for cp in outs:
        cp.wait()


def body(snapshots, start_basis, start_moments, station_power, girth_power, slab_id, slab_scale):
    dma = pltpu.SemaphoreType.DMA
    any_spec = pl.BlockSpec(memory_space=pl.ANY)
    vmem = pl.BlockSpec(memory_space=pltpu.VMEM)
    low = lambda *shape: pltpu.VMEM(shape, LOW)
    wide = lambda *shape: pltpu.VMEM(shape, F32)
    return pl.pallas_call(
        kernel,
        out_shape=(
            jax.ShapeDtypeStruct((ROWS, K, GIRTH), LOW),
            jax.ShapeDtypeStruct((K, K), F32),
            jax.ShapeDtypeStruct((DESIGNS, K), F32),
        ),
        in_specs=[any_spec, any_spec, vmem, vmem, vmem, vmem, pl.BlockSpec(memory_space=pltpu.SMEM)],
        out_specs=(any_spec, vmem, vmem),
        scratch_shapes=[
            low(PARTS, DESIGNS, ROWS, WIDE),
            low(ROWS, DESIGNS, GIRTH),
            low(ROWS, 2 * K, GIRTH),
            wide(DESIGNS, 2 * K),
            wide(DESIGNS, 2 * K),
            wide(16, ROWS, 2 * K),
            wide(DESIGNS, 2 * K),
            low(K, GIRTH),
            low(PARTS, 8, K, WIDE),
            low(PARTS, 8, K, WIDE),
            wide(PARTS, 8, K, WIDE),
            low(PARTS, 8, K, WIDE),
            low(PARTS, 3, 2, K, WIDE),
            low(PARTS, 2, K, WIDE),
            low(PARTS, 2, K, WIDE),
            low(PARTS, ROWS, K, WIDE),
            low(ROWS, K, GIRTH),
            wide(2, K // 2, 2 * K),
            wide(4, K // 2, 2 * K),
            wide(2, K // 2, 2 * K),
            wide(8, K // 2, 2 * K),
            wide(4, K // 2, 2 * K),
            wide(4, K // 2, 2 * K),
            wide(K, K),
            dma((PARTS + 1,)),
            dma((16,)), dma((16,)),
            dma((16,)), dma((16,)),
            dma((PARTS,)), dma((PARTS,)),
            dma((PARTS, 3)), dma((PARTS, 3)),
            dma((PARTS,)), dma((PARTS,)),
            dma((PARTS, 3)), dma((PARTS, 3)),
            dma((PARTS, 4)), dma((PARTS, 4)),
            dma((5,)), dma((5,)),
            dma((14,)), dma((14,)),
            dma((4,)),
        ],
        compiler_params=pltpu.CompilerParams(
            collective_id=0, has_side_effects=True, vmem_limit_bytes=60 << 20
        ),
    )(
        snapshots, start_basis, start_moments,
        station_power.reshape(1, K), girth_power.reshape(1, K),
        slab_id.reshape(1, DESIGNS), slab_scale,
    )


def solution(mesh):
    in_specs = (
        P("design", "offset", None),
        P("offset", None, None),
        P(),
        P(),
        P(),
        P("design"),
        P(),
    )
    out_specs = (P("offset", None, None), P(), P("design", None))
    return jax.shard_map(body, mesh=mesh, in_specs=in_specs, out_specs=out_specs, check_vma=False)
```

time: 514 us -> 89.9 us (0.17)
  the two profiles are of different devices: /device:TPU:0 before, /device:TPU:1 now
where the time goes in v1:
time: 89.9 us; the launch traced here: 89.7 us
  Pallas kernels  83.6 us (93%)
  local copies, waits for them, and re-layouts  5.38 us (6%)
    pallas_call x1, Pallas kernels, body(): pl.pallas_call(kernel, out_shape=(jax.ShapeDtypeStruct((ROWS, K, GIRTH),...  83.6 us
    unnamed x4, local copies, waits for them, and re-layouts  3.77 us

profile of v1, /device:TPU:1, one launch (start us, length us, event | category | flops | bytes accessed | tf_op | source)
XLA Modules:
  0.0 89.7 jit_solution(3611795192618756693)
XLA Ops:
  0.6 83.6 %shard_map.94 = (bf16[16,64,1024]{2,1,0:T(8,128)(2,1)}, f32[64,64]{1,0:T(8,128)}, f32[256,64]{1,0:T(8,128)}) custom-call(bf16[256,16,1024]{2,1,0:T(8,128)(2,1)} %snap_hbm.1, bf16[16,64,1024]{2,1,0:T(8,128)(2,1)} %start_hbm.1, f32[64,64]{1,0:T(8,128)} %moments_ref.1, s32[1,64]{1,0:T(1,128)} %bitcast.4, s32[1,64]{1,0:T(1,128)} %bitcast.5, s32[1,256]{1,0:T(1,128)} %bitcast.3, ...), custom_call_target="tpu_custom_call" | custom-call | tf_op jit(solution)/shard_map/pallas_call | solution.py:446
  84.3 1.6 %copy.10 = f32[256,64]{0,1:T(8,128)} copy(f32[256,64]{1,0:T(8,128)} %get-tuple-element.5) | data formatting | bytes 131072 | tf_op jit(solution)/shard_map/pallas_call | solution.py:446
  85.9 0.0 copy-start
  85.9 3.1 %copy.13 = bf16[16,64,1024]{2,1,0:T(8,128)(2,1)} copy(bf16[16,64,1024]{2,1,0:T(8,128)(2,1)} %get-tuple-element.9) | data formatting | bytes 4194304
  89.0 0.0 copy-done
  89.0 0.6 copy.14
Async XLA Ops:
  85.9 3.2 %copy-start = (f32[64,64]{1,0:T(8,128)S(1)}, f32[64,64]{1,0:T(8,128)}, u32[]{:S(2)}) copy-start(f32[64,64]{1,0:T(8,128)} %get-tuple-element.10) | copy-start | bytes 49156

commit v2 on v1

--- a/solution.py
+++ b/solution.py
@@ -40,12 +40,15 @@
     return jnp.where(powers == 4, square * square, out)
 
 
-def inverse_factor(matrix):
+def inverse_factor(matrix, hooks=()):
     eye = (iota((K, K), 0) == iota((K, K), 1)).astype(F32)
     both = jnp.concatenate([matrix, eye], axis=1)
     blocks = [both[8 * b : 8 * b + 8] for b in range(K // 8)]
     sub = iota((8, 1), 0)
+    hooks = dict(hooks)
     for j in range(K):
+        if j in hooks:
+            hooks[j]()
         b, r = j // 8, j % 8
         row = blocks[b][r : r + 1, :]
         row = row / row[:, j : j + 1]
@@ -76,13 +79,14 @@
 
 def kernel(
     snap_hbm, start_hbm, moments_ref, spow_ref, gpow_ref, slab_ref, slab_scale,
-    basis_hbm, basis_moments_ref, moments_out,
-    raw, turned, weights, acc, scale_ref, parts_ref, coords_ref, girth_ref,
-    core_out, core_in, mine, y_out, y_in, z_out, z_in, full, result,
-    im_core, im_y, im_z, gram_1, gram_2, gram_3, gram_total,
+    full, inverse_out, basis_moments_out, moments_out,
+    raw, turned_0, turned_1, turned_2, turned_3, weights, acc, scale_ref, parts_ref, coords_ref, girth_ref,
+    core_out, core_in, mine, y_out, y_in, z_out, z_in, image_ref,
+    im_core, im_y, im_z, gram_1, gram_2, gram_3,
     load_sem, part_s, part_r, coord_s, coord_r, core_s, core_r, y_s, y_r, z_s, z_r,
-    g_s, g_r, f_s, f_r, im_s, im_r, gr_s, gr_r, out_sem,
+    g_s, g_r, f_s, f_r, im_s, im_r, gr_s, gr_r, own_sem,
 ):
+    turned = (turned_0, turned_1, turned_2, turned_3)
     de, of = lax.axis_index("design"), lax.axis_index("offset")
     c, y, zh = lax.rem(de, 2), lax.rem(de // 2, 4), de // 8
     zl, x = of // 4, lax.rem(of, 4)
@@ -138,54 +142,6 @@
     scale = column(scale / 512.0, 2 * K)
     scale_ref[...] = jnp.where(iota((DESIGNS, 2 * K), 1) < K, 1.0, scale)
 
-    lane_power = jnp.concatenate([jnp.zeros((1, K), jnp.int32), spow], axis=1)
-    acc[...] = jnp.zeros_like(acc)
-    for q in range(PARTS):
-        loads[q].wait()
-
-        @pl.loop(0, DESIGNS // 16)
-        def _(i):
-            d0 = pl.multiple_of(i * 16, 16)
-            for g in range(WIDE // 128):
-                v = raw[q, pl.ds(d0, 16), :, pl.ds(g * 128, 128)]
-                turned[:, pl.ds(d0, 16), pl.ds(q * WIDE + g * 128, 128)] = jnp.swapaxes(v, 0, 1)
-
-        if q == 0:
-            start_load.wait()
-
-        @pl.loop(0, ROWS // 4)
-        def _(i):
-            total = acc[...]
-            for j in range(4):
-                s = i * 4 + j
-                t = ((of * ROWS + s).astype(F32) + 0.5) / STATIONS
-                lanes = pl.ds(q * WIDE, WIDE)
-                part = lax.dot_general(
-                    turned[s, :, lanes], weights[s, :, lanes], (((1,), (1,)), ((), ())),
-                    preferred_element_type=F32,
-                )
-                total = total + part * power_of(t, lane_power)
-            acc[...] = total
-
-    pl.semaphore_wait(barrier, 30)
-
-    def row_block(of_):
-        return pl.ds(pl.multiple_of(of_ * ROWS, ROWS), ROWS)
-
-    def part_copy(r):
-        to = lax.rem(of + r, 16)
-        return copy(acc.at[row_block(to)], parts_ref.at[of], part_s.at[r], part_r.at[of], (de, to))
-
-    def part_arrival(r):
-        frm = lax.rem(of + r, 16)
-        return copy(acc.at[row_block(of)], parts_ref.at[frm], part_s.at[r], part_r.at[frm], (de, frm))
-
-    @pl.loop(1, 16)
-    def _(r):
-        part_copy(r).start()
-
-    parts_ref[of] = acc[row_block(of), :]
-
     pc = column(spow.astype(F32), K) + spow.astype(F32)
     qc = column(gpow.astype(F32), K) + gpow.astype(F32)
     even = lax.rem(qc.astype(jnp.int32), 2) == 0
@@ -197,6 +153,57 @@
     )
     eye = iota((K, K), 0) == iota((K, K), 1)
     model = model + jnp.where(eye, 1.0, 0.0)
+
+    lane_power = jnp.concatenate([jnp.zeros((1, K), jnp.int32), spow], axis=1)
+    acc[...] = jnp.zeros_like(acc)
+
+    def stand(q, i):
+        d0 = pl.multiple_of(i * 16, 16)
+        for g in range(WIDE // 128):
+            lanes = pl.ds(g * 128, 128)
+            turned[q][:, pl.ds(d0, 16), lanes] = jnp.swapaxes(raw[q, pl.ds(d0, 16), :, lanes], 0, 1)
+
+    loads[0].wait()
+
+    for i in range(16):
+        stand(0, i)
+
+    start_load.wait()
+    for q in range(PARTS):
+        if q + 1 < PARTS:
+            loads[q + 1].wait()
+
+        total = acc[...]
+        for s in range(ROWS):
+            t = ((of * ROWS + s).astype(F32) + 0.5) / STATIONS
+            part = lax.dot_general(
+                turned[q][s], weights[s, :, pl.ds(q * WIDE, WIDE)], (((1,), (1,)), ((), ())),
+                preferred_element_type=F32,
+            )
+            total = total + part * power_of(t, lane_power)
+            if q + 1 < PARTS:
+                stand(q + 1, s)
+        acc[...] = total
+
+    pl.semaphore_wait(barrier, 30)
+
+    def row_block(of_):
+        return pl.ds(pl.multiple_of(of_ * ROWS, ROWS), ROWS)
+
+    def part_copy(r):
+        to = lax.rem(of + r, 16)
+        return copy(acc.at[row_block(to)], parts_ref.at[of], part_s.at[r], part_r.at[of], (de, to))
+
+    def part_arrival(r):
+        frm = lax.rem(of + r, 16)
+        return copy(acc.at[row_block(of)], parts_ref.at[frm], part_s.at[r], part_r.at[frm], (de, frm))
+
+    @pl.loop(1, 16)
+    def _(r):
+        part_copy(r).start()
+
+    parts_ref[of] = acc[row_block(of), :]
+
     turn = inverse_factor(model)
 
     @pl.loop(1, 16)
@@ -241,8 +248,9 @@
 
     coords = coords_ref[:, :K]
     moments = coords_ref[:, K:]
-    moments_out[...] = moments
-    tall = jnp.transpose(coords_ref[...])[:K].astype(LOW)
+    upright = jnp.transpose(coords_ref[...])
+    moments_out[...] = upright[K:]
+    tall = upright[:K].astype(LOW)
 
     pending = []
 
@@ -258,33 +266,22 @@
     im_core[0] = fold(images_moments)
 
     def images(q):
-        lanes = pl.ds(q * WIDE, WIDE)
-
-        @pl.loop(0, 2)
-        def _(i):
-            for j in range(4):
-                n = i * 4 + j
-                core_out[q, n] = jnp.dot(
-                    tall, turned[(1 - c) * 8 + n, :, lanes], preferred_element_type=F32
-                ).astype(LOW)
+        for n in range(8):
+            core_out[q, n] = jnp.dot(
+                tall, turned[q][(1 - c) * 8 + n], preferred_element_type=F32
+            ).astype(LOW)
 
         cp = send(core_out.at[q], core_in.at[q], core_s.at[q], core_r.at[q], sibling)
 
-        @pl.loop(0, 2)
-        def _(i):
-            for j in range(4):
-                n = i * 4 + j
-                mine[q, n] = jnp.dot(
-                    tall, turned[c * 8 + n, :, lanes], preferred_element_type=F32
-                )
+        for n in range(8):
+            mine[q, n] = jnp.dot(tall, turned[q][c * 8 + n], preferred_element_type=F32)
 
         return cp
 
     def to_y(q, cp):
         cp.wait_recv()
 
-        @pl.loop(0, 8)
-        def _(n):
+        for n in range(8):
             y_out[q, n] = (mine[q, n] + core_in[q, n].astype(F32)).astype(LOW)
 
         cps = []
@@ -308,23 +305,31 @@
 
     first = c * 8 + 2 * y
 
-    def gather(q, cp, gram):
+    def settle(q, cp, gram):
         cp.wait_recv()
         for h in range(2):
             image = (z_out[q, h].astype(F32) + z_in[q, h].astype(F32)).astype(LOW)
-            full[q, first + h] = image
+            image_ref[q, h] = image
             gram = gram + lax.dot_general(
                 image, image, (((1,), (1,)), ((), ())), preferred_element_type=F32
             )
+        return gram
+
+    own = []
+
+    def gather(q):
         pair = full.at[q, pl.ds(first, 2)]
         cps = [
-            send(pair, pair, g_s.at[q, r - 1], g_r.at[q, r - 1], along_y(r)) for r in (2, 1, 3)
+            send(image_ref.at[q], pair, g_s.at[q, r - 1], g_r.at[q, r - 1], along_y(r))
+            for r in (2, 1, 3)
         ]
-        cps.append(send(pair, pair, f_s.at[q, 0], f_r.at[q, 0], sibling))
-        return cps, gram
-
-    def hand_on(q, cps):
-        for cp, r in zip(cps[:3], (2, 1, 3)):
+        send(image_ref.at[q], pair, f_s.at[q, 0], f_r.at[q, 0], sibling)
+        own.append(pltpu.make_async_copy(image_ref.at[q], pair, own_sem.at[q]))
+        own[-1].start()
+        return cps
+
+    def hand_on(q):
+        for cp, r in zip(g_cp[q], (2, 1, 3)):
             cp.wait_recv()
             frm = lax.rem(y + 4 - r, 4)
             pair = full.at[q, pl.ds(c * 8 + 2 * frm, 2)]
@@ -336,78 +341,81 @@
             cps.append(send(ref.at[slot], ref.at[slot], gr_s.at[sems + r], gr_r.at[sems + r], to))
         return cps
 
-    core_im = send(im_core.at[0], im_core.at[1], im_s.at[0], im_r.at[0], sibling)
     core_cp = [None] * PARTS
     y_cp = [None] * PARTS
     z_cp = [None] * PARTS
     g_cp = [None] * PARTS
     core_cp[0] = images(0)
+    core_im = send(im_core.at[0], im_core.at[1], im_s.at[0], im_r.at[0], sibling)
     core_cp[1] = images(1)
     y_cp[0] = to_y(0, core_cp[0])
     core_cp[2] = images(2)
     y_cp[1] = to_y(1, core_cp[1])
+    core_cp[3] = images(3)
     core_im.wait_recv()
     im_y[y] = im_core[0] + im_core[1]
     im_cps = [
         send(im_y.at[y], im_y.at[y], im_s.at[r], im_r.at[r], along_y(r)) for r in (1, 2, 3)
     ]
-    core_cp[3] = images(3)
+    z_cp[0] = to_z(0, y_cp[0])
     y_cp[2] = to_y(2, core_cp[2])
-    y_cp[3] = to_y(3, core_cp[3])
     for cp in im_cps:
         cp.wait_recv()
     im_z[0] = (im_y[0] + im_y[1]) + (im_y[2] + im_y[3])
     im_cp = send(im_z.at[0], im_z.at[1], im_s.at[4], im_r.at[4], beyond)
+    z_cp[1] = to_z(1, y_cp[1])
+    y_cp[3] = to_y(3, core_cp[3])
+    z_cp[2] = to_z(2, y_cp[2])
+    z_cp[3] = to_z(3, y_cp[3])
 
     gram = jnp.zeros((K, K), F32)
-    z_cp[0] = to_z(0, y_cp[0])
-    z_cp[1] = to_z(1, y_cp[1])
-    g_cp[0], gram = gather(0, z_cp[0], gram)
-    z_cp[2] = to_z(2, y_cp[2])
-    g_cp[1], gram = gather(1, z_cp[1], gram)
-    z_cp[3] = to_z(3, y_cp[3])
-    g_cp[2], gram = gather(2, z_cp[2], gram)
-    g_cp[3], gram = gather(3, z_cp[3], gram)
+    gram = settle(0, z_cp[0], gram)
+    g_cp[0] = gather(0)
+    gram = settle(1, z_cp[1], gram)
+    g_cp[1] = gather(1)
+    im_cp.wait_recv()
+    images_moments = unfold(im_z[0] + im_z[1])
+    moments_part = lax.dot_general(
+        images_moments, images_moments, (((0,), (0,)), ((), ())),
+        precision=HIGH, preferred_element_type=F32,
+    )
+    gram = settle(2, z_cp[2], gram)
+    gram = settle(3, z_cp[3], gram)
 
     me = 2 * y + c
     gram_1[me] = fold(gram)
     cps = []
     for r in range(1, 8):
-        ry, rc = r // 2, r % 2
-        to = at(zh, lax.rem(y + ry, 4), lax.rem(c + rc, 2))
+        to = at(zh, lax.rem(y + r // 2, 4), lax.rem(c + r % 2, 2))
         cps.append((r, to))
     cps = exchange(gram_1, me, cps, 0)
-    im_cp.wait_recv()
-    images_moments = unfold(im_z[0] + im_z[1])
-    hand_on(0, g_cp[0])
+    g_cp[2] = gather(2)
+    g_cp[3] = gather(3)
     for cp in cps:
         cp.wait_recv()
     total = gram_1[0]
     for j in range(1, 8):
         total = total + gram_1[j]
     gram_2[x] = total
-    cps = exchange(gram_2, x, [(r, (de, zl * 4 + lax.rem(x + r, 4))) for r in (1, 2, 3)], 7)
+    cps = exchange(gram_2, x, [(r, (de, zl * 4 + lax.rem(x + r, 4))) for r in (2, 1, 3)], 7)
+    hand_on(0)
     for cp in cps:
         cp.wait_recv()
     gram_3[zl] = (gram_2[0] + gram_2[1]) + (gram_2[2] + gram_2[3])
-    cps = exchange(gram_3, zl, [(r, (de, lax.rem(zl + r, 4) * 4 + x)) for r in (1, 2, 3)], 10)
-    hand_on(1, g_cp[1])
+    cps = exchange(gram_3, zl, [(r, (de, lax.rem(zl + r, 4) * 4 + x)) for r in (2, 1, 3)], 10)
+    hand_on(1)
     for cp in cps:
         cp.wait_recv()
-    gram = unfold((gram_3[0] + gram_3[1]) + (gram_3[2] + gram_3[3]))
-    gram = gram + lax.dot_general(
-        images_moments, images_moments, (((0,), (0,)), ((), ())),
-        precision=HIGH, preferred_element_type=F32,
-    )
-    inverse = inverse_factor(gram / (STATIONS * GIRTH))
-    hand_on(2, g_cp[2])
-    hand_on(3, g_cp[3])
-    basis_moments_ref[...] = lax.dot_general(
+    gram = unfold((gram_3[0] + gram_3[1]) + (gram_3[2] + gram_3[3])) + moments_part
+    inverse = inverse_factor(
+        gram / (STATIONS * GIRTH), [(24, lambda: hand_on(2)), (48, lambda: hand_on(3))]
+    )
+    basis_moments_out[...] = lax.dot_general(
         images_moments, inverse, (((1,), (1,)), ((), ())),
         precision=HIGH, preferred_element_type=F32,
     )
     high = inverse.astype(LOW)
-    pieces = jnp.concatenate([high, (inverse - high.astype(F32)).astype(LOW)], axis=0)
+    inverse_out[...] = jnp.concatenate([high, (inverse - high.astype(F32)).astype(LOW)], axis=0)
 
     for q in range(PARTS):
         for r in range(4):
@@ -415,17 +423,6 @@
             pair = full.at[q, pl.ds((1 - c) * 8 + 2 * frm, 2)]
             copy(pair, pair, f_s.at[q, r], f_r.at[q, r], sibling).wait_recv()
 
-    outs = []
-    for i in range(4):
-        for j in range(4):
-            s = i * 4 + j
-            for q in range(PARTS):
-                out = jnp.dot(pieces, full[q, s], preferred_element_type=F32)
-                result[s, :, pl.ds(q * WIDE, WIDE)] = (out[:K] + out[K:]).astype(LOW)
-        block = pl.ds(i * 4, 4)
-        outs.append(pltpu.make_async_copy(result.at[block], basis_hbm.at[block], out_sem.at[i]))
-        outs[-1].start()
-
     @pl.loop(1, 16)
     def _(r):
         part_copy(r).wait_send()
@@ -433,6 +430,39 @@
 
     for cp in pending:
         cp.wait_send()
+    for cp in own:
+        cp.wait()
+
+
+def finish(
+    full, pieces_ref, basis_moments_in, moments_in, basis_hbm, basis_moments_ref, moments_ref,
+    images, result, in_sem, out_sem, small_sem,
+):
+    loads = [
+        pltpu.make_async_copy(full.at[q], images.at[q], in_sem.at[q]) for q in range(PARTS)
+    ]
+    for cp in loads:
+        cp.start()
+    outs = [
+        pltpu.make_async_copy(basis_moments_in, basis_moments_ref, small_sem.at[0]),
+        pltpu.make_async_copy(moments_in, moments_ref, small_sem.at[1]),
+    ]
+    for cp in outs:
+        cp.start()
+    pieces = pieces_ref[...]
+    for q in range(PARTS):
+        loads[q].wait()
+
+        for s in range(ROWS):
+            out = jnp.dot(pieces, images[q, s], preferred_element_type=F32)
+            result[q, s] = (out[:K] + out[K:]).astype(LOW)
+
+        outs.append(
+            pltpu.make_async_copy(
+                result.at[q], basis_hbm.at[:, :, pl.ds(q * WIDE, WIDE)], out_sem.at[q]
+            )
+        )
+        outs[-1].start()
     for cp in outs:
         cp.wait()
 
@@ -443,18 +473,19 @@
     vmem = pl.BlockSpec(memory_space=pltpu.VMEM)
     low = lambda *shape: pltpu.VMEM(shape, LOW)
     wide = lambda *shape: pltpu.VMEM(shape, F32)
-    return pl.pallas_call(
+    full, pieces, basis_moments, moments = pl.pallas_call(
         kernel,
         out_shape=(
-            jax.ShapeDtypeStruct((ROWS, K, GIRTH), LOW),
+            jax.ShapeDtypeStruct((PARTS, ROWS, K, WIDE), LOW),
+            jax.ShapeDtypeStruct((2 * K, K), LOW),
             jax.ShapeDtypeStruct((K, K), F32),
-            jax.ShapeDtypeStruct((DESIGNS, K), F32),
+            jax.ShapeDtypeStruct((K, DESIGNS), F32),
         ),
         in_specs=[any_spec, any_spec, vmem, vmem, vmem, vmem, pl.BlockSpec(memory_space=pltpu.SMEM)],
-        out_specs=(any_spec, vmem, vmem),
+        out_specs=(any_spec, vmem, vmem, vmem),
         scratch_shapes=[
             low(PARTS, DESIGNS, ROWS, WIDE),
-            low(ROWS, DESIGNS, GIRTH),
+            *[low(ROWS, DESIGNS, WIDE)] * PARTS,
             low(ROWS, 2 * K, GIRTH),
             wide(DESIGNS, 2 * K),
             wide(DESIGNS, 2 * K),
@@ -468,15 +499,13 @@
             low(PARTS, 3, 2, K, WIDE),
             low(PARTS, 2, K, WIDE),
             low(PARTS, 2, K, WIDE),
-            low(PARTS, ROWS, K, WIDE),
-            low(ROWS, K, GIRTH),
+            low(PARTS, 2, K, WIDE),
             wide(2, K // 2, 2 * K),
             wide(4, K // 2, 2 * K),
             wide(2, K // 2, 2 * K),
             wide(8, K // 2, 2 * K),
             wide(4, K // 2, 2 * K),
             wide(4, K // 2, 2 * K),
-            wide(K, K),
             dma((PARTS + 1,)),
             dma((16,)), dma((16,)),
             dma((16,)), dma((16,)),
@@ -497,6 +526,23 @@
         station_power.reshape(1, K), girth_power.reshape(1, K),
         slab_id.reshape(1, DESIGNS), slab_scale,
     )
+    basis, basis_moments, moments = pl.pallas_call(
+        finish,
+        out_shape=(
+            jax.ShapeDtypeStruct((ROWS, K, GIRTH), LOW),
+            jax.ShapeDtypeStruct((K, K), F32),
+            jax.ShapeDtypeStruct((K, DESIGNS), F32),
+        ),
+        in_specs=[any_spec, vmem, any_spec, any_spec],
+        out_specs=(any_spec, any_spec, any_spec),
+        scratch_shapes=[
+            low(PARTS, ROWS, K, WIDE),
+            low(PARTS, ROWS, K, WIDE),
+            dma((PARTS,)), dma((PARTS,)), dma((2,)),
+        ],
+        compiler_params=pltpu.CompilerParams(vmem_limit_bytes=60 << 20),
+    )(full, pieces, basis_moments, moments)
+    return basis, basis_moments, moments.T
 
 
 def solution(mesh):

time: 89.9 us -> 77.9 us (0.87)
  Pallas kernels: 83.6 us -> 77 us
  local copies, waits for them, and re-layouts: 5.38 us -> 0 us
    pallas_call x1 -> x2, Pallas kernels: 83.6 us -> 77 us  [the longest x1 72.1 us: body(): pl.pallas_call(kernel, out_shape=(jax.ShapeDtypeStruct((PARTS, ROWS, K, W...]
    unnamed x4 -> x0, local copies, waits for them, and re-layouts: 3.77 us -> none
    pallas_call x1 -> x0, local copies, waits for them, and re-layouts: 1.62 us -> none  [body(): pl.pallas_call(kernel, out_shape=(jax.ShapeDtypeStruct((ROWS, K, GIRTH),...]
where the time goes in v2:
time: 77.9 us; the launch traced here: 77.7 us
  Pallas kernels  77 us (99%)
    pallas_call x1, Pallas kernels, body(): pl.pallas_call(kernel, out_shape=(jax.ShapeDtypeStruct((PARTS, ROWS, K, W...  72.1 us
    pallas_call x1, Pallas kernels, body(): pl.pallas_call(finish, out_shape=(jax.ShapeDtypeStruct((ROWS, K, GIRTH),...  4.93 us

profile of v2, /device:TPU:1, one launch (start us, length us, event | category | flops | bytes accessed | tf_op | source)
XLA Modules:
  0.0 77.7 jit_solution(899807906235390289)
XLA Ops:
  0.6 72.1 %shard_map.94 = (bf16[4,16,64,256]{3,2,1,0:T(8,128)(2,1)}, bf16[128,64]{1,0:T(8,128)(2,1)}, f32[64,64]{1,0:T(8,128)}, f32[64,256]{1,0:T(8,128)}) custom-call(bf16[256,16,1024]{2,1,0:T(8,128)(2,1)} %snap_hbm.1, bf16[16,64,1024]{2,1,0:T(8,128)(2,1)} %start_hbm.1, f32[64,64]{1,0:T(8,128)} %moments_ref.1, s32[1,64]{1,0:T(1,128)} %bitcast.5, s32[1,64]{1,0:T(1,128)} %bitcast.6, ...), custom_call_target="tpu_custom_call" | custom-call | tf_op jit(solution)/shard_map/pallas_call | solution.py:476
  72.7 4.9 %shard_map.95 = (bf16[16,64,1024]{2,1,0:T(8,128)(2,1)}, f32[64,64]{1,0:T(8,128)}, f32[64,256]{1,0:T(8,128)}) custom-call(bf16[4,16,64,256]{3,2,1,0:T(8,128)(2,1)} %get-tuple-element.10.full, bf16[128,64]{1,0:T(8,128)(2,1)} %get-tuple-element.11.pieces_ref, f32[64,64]{1,0:T(8,128)} %get-tuple-element.12.basis_moments_in, f32[64,256]{1,0:T(8,128)} %get-tuple-element.13.moments_in), custom_call_target="tpu_custom_call" | custom-call | tf_op jit(solution)/shard_map/pallas_call | solution.py:529

commit v3 on v2

--- a/solution.py
+++ b/solution.py
@@ -13,6 +13,8 @@
 DESIGNS = 256
 PARTS = 4
 WIDE = GIRTH // PARTS
+TRAVEL = 8
+NARROW = GIRTH // TRAVEL
 
 HIGH = lax.Precision.HIGHEST
 MESH = pl.DeviceIdType.MESH
@@ -78,13 +80,14 @@
 
 
 def kernel(
-    snap_hbm, start_hbm, moments_ref, spow_ref, gpow_ref, slab_ref, slab_scale,
+    snap_hbm, start_hbm, moments_hbm, spow_hbm, gpow_hbm, slab_hbm, slab_scale_hbm,
     full, inverse_out, basis_moments_out, moments_out,
+    moments_ref, spow_ref, gpow_ref, slab_ref, slab_scale_ref,
     raw, turned_0, turned_1, turned_2, turned_3, weights, acc, scale_ref, parts_ref, coords_ref, girth_ref,
     core_out, core_in, mine, y_out, y_in, z_out, z_in, image_ref,
     im_core, im_y, im_z, gram_1, gram_2, gram_3,
     load_sem, part_s, part_r, coord_s, coord_r, core_s, core_r, y_s, y_r, z_s, z_r,
-    g_s, g_r, f_s, f_r, im_s, im_r, gr_s, gr_r, own_sem,
+    g_s, g_r, f_s, f_r, im_s, im_r, gr_s, gr_r, own_sem, small_sem,
 ):
     turned = (turned_0, turned_1, turned_2, turned_3)
     de, of = lax.axis_index("design"), lax.axis_index("offset")
@@ -106,24 +109,46 @@
             device_id=to, device_id_type=MESH,
         )
 
-    barrier = pltpu.get_barrier_semaphore()
-
-    @pl.loop(1, 16)
-    def _(r):
-        pl.semaphore_signal(barrier, inc=1, device_id=(lax.rem(de + r, 16), of), device_id_type=MESH)
-        pl.semaphore_signal(barrier, inc=1, device_id=(de, lax.rem(of + r, 16)), device_id_type=MESH)
-
+    small = [
+        pltpu.make_async_copy(src, dst, small_sem.at[i])
+        for i, (src, dst) in enumerate(
+            (
+                (spow_hbm, spow_ref), (gpow_hbm, gpow_ref), (moments_hbm, moments_ref),
+                (slab_hbm, slab_ref), (slab_scale_hbm, slab_scale_ref),
+            )
+        )
+    ]
+    for cp in small:
+        cp.start()
     loads = []
     for q in range(PARTS):
         lanes = pl.ds(q * WIDE, WIDE)
         loads.append(pltpu.make_async_copy(snap_hbm.at[:, :, lanes], raw.at[q], load_sem.at[q]))
-        loads[-1].start()
+        if q < 2:
+            loads[-1].start()
         if q == 0:
             start_load = pltpu.make_async_copy(
                 start_hbm, weights.at[:, pl.ds(0, K), :], load_sem.at[PARTS]
             )
             start_load.start()
 
+    barrier = pltpu.get_barrier_semaphore()
+
+    @pl.loop(1, 16)
+    def _(r):
+        pl.semaphore_signal(barrier, inc=1, device_id=(lax.rem(de + r, 16), of), device_id_type=MESH)
+        pl.semaphore_signal(barrier, inc=1, device_id=(de, lax.rem(of + r, 16)), device_id_type=MESH)
+
+    def along_z(r):
+        z = lax.rem(zh * 4 + zl + r + 8, 8)
+        return ((z // 4) * 8 + lax.rem(de, 8), lax.rem(z, 4) * 4 + x)
+
+    for r in (1, -1, 2, -2):
+        pl.semaphore_signal(barrier, inc=1, device_id=along_z(r), device_id_type=MESH)
+
+    for cp in small:
+        cp.wait()
+
     spow = spow_ref[...]
     gpow = gpow_ref[...]
     u = (2.0 * (iota((K, GIRTH), 1).astype(F32) + 0.5)) / GIRTH - 1.0
@@ -134,11 +159,11 @@
         weights[s, pl.ds(K, K), :] = girth_ref[...]
 
     slab = slab_ref[...]
+    slab_scale = slab_scale_ref[...]
     scale = jnp.zeros((1, DESIGNS), F32)
-    square = jnp.float32(0.0)
+    square = jnp.sum(slab_scale * slab_scale, axis=1, keepdims=True)
     for j in range(SLABS):
-        scale = jnp.where(slab == j, slab_scale[j], scale)
-        square = square + slab_scale[j] * slab_scale[j]
+        scale = jnp.where(slab == j, slab_scale[:, j : j + 1], scale)
     scale = column(scale / 512.0, 2 * K)
     scale_ref[...] = jnp.where(iota((DESIGNS, 2 * K), 1) < K, 1.0, scale)
 
@@ -163,29 +188,36 @@
             lanes = pl.ds(g * 128, 128)
             turned[q][:, pl.ds(d0, 16), lanes] = jnp.swapaxes(raw[q, pl.ds(d0, 16), :, lanes], 0, 1)
 
-    loads[0].wait()
-
-    for i in range(16):
-        stand(0, i)
-
+    def dots(q, total, s):
+        t = ((of * ROWS + s).astype(F32) + 0.5) / STATIONS
+        part = lax.dot_general(
+            jnp.concatenate([turned[q][s], turned[q + 1][s]], axis=1),
+            weights[s, :, pl.ds(q * WIDE, 2 * WIDE)], (((1,), (1,)), ((), ())),
+            preferred_element_type=F32,
+        )
+        return total + part * power_of(t, lane_power)
+
+    for q in range(2):
+        loads[q].wait()
+        if q + 2 < PARTS:
+            loads[q + 2].start()
+        for i in range(16):
+            stand(q, i)
     start_load.wait()
-    for q in range(PARTS):
-        if q + 1 < PARTS:
-            loads[q + 1].wait()
-
-        total = acc[...]
-        for s in range(ROWS):
-            t = ((of * ROWS + s).astype(F32) + 0.5) / STATIONS
-            part = lax.dot_general(
-                turned[q][s], weights[s, :, pl.ds(q * WIDE, WIDE)], (((1,), (1,)), ((), ())),
-                preferred_element_type=F32,
-            )
-            total = total + part * power_of(t, lane_power)
-            if q + 1 < PARTS:
-                stand(q + 1, s)
-        acc[...] = total
-
-    pl.semaphore_wait(barrier, 30)
+    total = jnp.zeros((DESIGNS, 2 * K), F32)
+    for q in range(2, 4):
+        loads[q].wait()
+        if q + 2 < PARTS:
+            loads[q + 2].start()
+        for i in range(16):
+            stand(q, i)
+            if i % 2 == 0:
+                total = dots(0, total, (q - 2) * 8 + i // 2)
+    for s in range(ROWS):
+        total = dots(2, total, s)
+    acc[...] = total
+
+    pl.semaphore_wait(barrier, 34)
 
     def row_block(of_):
         return pl.ds(pl.multiple_of(of_ * ROWS, ROWS), ROWS)
@@ -260,11 +292,6 @@
         pending.append(cp)
         return cp
 
-    images_moments = lax.dot_general(
-        moments, coords, (((0,), (0,)), ((), ())), precision=HIGH, preferred_element_type=F32
-    )
-    im_core[0] = fold(images_moments)
-
     def images(q):
         for n in range(8):
             core_out[q, n] = jnp.dot(
@@ -278,38 +305,43 @@
 
         return cp
 
-    def to_y(q, cp):
-        cp.wait_recv()
-
+    def place(p):
+        return p * NARROW // WIDE, pl.ds(p * NARROW % WIDE, NARROW)
+
+    def to_y(p):
+        q, lanes = place(p)
+        if p * NARROW % WIDE == 0:
+            core_cp[q].wait_recv()
         for n in range(8):
-            y_out[q, n] = (mine[q, n] + core_in[q, n].astype(F32)).astype(LOW)
-
+            y_out[p, n] = (mine[q, n, :, lanes] + core_in[q, n, :, lanes].astype(F32)).astype(LOW)
         cps = []
         for r in (2, 1, 3):
             pair = pl.ds(2 * lax.rem(y + r, 4), 2)
             cps.append(
-                send(y_out.at[q, pair], y_in.at[q, r - 1], y_s.at[q, r - 1], y_r.at[q, r - 1], along_y(r))
+                send(y_out.at[p, pair], y_in.at[p, r - 1], y_s.at[p, r - 1], y_r.at[p, r - 1], along_y(r))
             )
-        return cps
-
-    def to_z(q, cps):
-        for cp in cps:
+        y_cp[p] = cps
+
+    def to_z(p):
+        q, lanes = place(p)
+        for cp in y_cp[p]:
             cp.wait_recv()
         for h in range(2):
             n = 2 * y + h
-            total = mine[q, n] + core_in[q, n].astype(F32)
+            total = mine[q, n, :, lanes] + core_in[q, n, :, lanes].astype(F32)
             for r in range(3):
-                total = total + y_in[q, r, h].astype(F32)
-            z_out[q, h] = total.astype(LOW)
-        return send(z_out.at[q], z_in.at[q], z_s.at[q], z_r.at[q], beyond)
+                total = total + y_in[p, r, h].astype(F32)
+            z_out[p, h] = total.astype(LOW)
+        z_cp[p] = send(z_out.at[p], z_in.at[p], z_s.at[p], z_r.at[p], beyond)
 
     first = c * 8 + 2 * y
 
-    def settle(q, cp, gram):
-        cp.wait_recv()
+    def settle(p, gram):
+        q, lanes = place(p)
+        z_cp[p].wait_recv()
         for h in range(2):
-            image = (z_out[q, h].astype(F32) + z_in[q, h].astype(F32)).astype(LOW)
-            image_ref[q, h] = image
+            image = (z_out[p, h].astype(F32) + z_in[p, h].astype(F32)).astype(LOW)
+            image_ref[q, h, :, lanes] = image
             gram = gram + lax.dot_general(
                 image, image, (((1,), (1,)), ((), ())), preferred_element_type=F32
             )
@@ -342,36 +374,45 @@
         return cps
 
     core_cp = [None] * PARTS
-    y_cp = [None] * PARTS
-    z_cp = [None] * PARTS
+    y_cp = [None] * TRAVEL
+    z_cp = [None] * TRAVEL
     g_cp = [None] * PARTS
+    per = TRAVEL // PARTS
     core_cp[0] = images(0)
+    core_cp[1] = images(1)
+    for p in range(per):
+        to_y(p)
+    core_cp[2] = images(2)
+    for p in range(per, 2 * per):
+        to_y(p)
+    core_cp[3] = images(3)
+    images_moments = lax.dot_general(
+        moments, coords, (((0,), (0,)), ((), ())), precision=HIGH, preferred_element_type=F32
+    )
+    im_core[0] = fold(images_moments)
     core_im = send(im_core.at[0], im_core.at[1], im_s.at[0], im_r.at[0], sibling)
-    core_cp[1] = images(1)
-    y_cp[0] = to_y(0, core_cp[0])
-    core_cp[2] = images(2)
-    y_cp[1] = to_y(1, core_cp[1])
-    core_cp[3] = images(3)
-    core_im.wait_recv()
-    im_y[y] = im_core[0] + im_core[1]
-    im_cps = [
-        send(im_y.at[y], im_y.at[y], im_s.at[r], im_r.at[r], along_y(r)) for r in (1, 2, 3)
-    ]
-    z_cp[0] = to_z(0, y_cp[0])
-    y_cp[2] = to_y(2, core_cp[2])
-    for cp in im_cps:
-        cp.wait_recv()
-    im_z[0] = (im_y[0] + im_y[1]) + (im_y[2] + im_y[3])
-    im_cp = send(im_z.at[0], im_z.at[1], im_s.at[4], im_r.at[4], beyond)
-    z_cp[1] = to_z(1, y_cp[1])
-    y_cp[3] = to_y(3, core_cp[3])
-    z_cp[2] = to_z(2, y_cp[2])
-    z_cp[3] = to_z(3, y_cp[3])
+    for p in range(TRAVEL):
+        to_z(p)
+        if p + 2 * per < TRAVEL:
+            to_y(p + 2 * per)
+        if p == 0:
+            core_im.wait_recv()
+            im_y[y] = im_core[0] + im_core[1]
+            im_cps = [
+                send(im_y.at[y], im_y.at[y], im_s.at[r], im_r.at[r], along_y(r)) for r in (1, 2, 3)
+            ]
+        if p == TRAVEL - 2:
+            for cp in im_cps:
+                cp.wait_recv()
+            im_z[0] = (im_y[0] + im_y[1]) + (im_y[2] + im_y[3])
+            im_cp = send(im_z.at[0], im_z.at[1], im_s.at[4], im_r.at[4], beyond)
 
     gram = jnp.zeros((K, K), F32)
-    gram = settle(0, z_cp[0], gram)
+    for p in range(per):
+        gram = settle(p, gram)
     g_cp[0] = gather(0)
-    gram = settle(1, z_cp[1], gram)
+    for p in range(per, 2 * per):
+        gram = settle(p, gram)
     g_cp[1] = gather(1)
     im_cp.wait_recv()
     images_moments = unfold(im_z[0] + im_z[1])
@@ -379,8 +420,8 @@
         images_moments, images_moments, (((0,), (0,)), ((), ())),
         precision=HIGH, preferred_element_type=F32,
     )
-    gram = settle(2, z_cp[2], gram)
-    gram = settle(3, z_cp[3], gram)
+    for p in range(2 * per, TRAVEL):
+        gram = settle(p, gram)
 
     me = 2 * y + c
     gram_1[me] = fold(gram)
@@ -402,7 +443,7 @@
     for cp in cps:
         cp.wait_recv()
     gram_3[zl] = (gram_2[0] + gram_2[1]) + (gram_2[2] + gram_2[3])
-    cps = exchange(gram_3, zl, [(r, (de, lax.rem(zl + r, 4) * 4 + x)) for r in (2, 1, 3)], 10)
+    cps = exchange(gram_3, zl, [(r, along_z(d)) for r, d in ((2, 2), (1, 1), (3, -1))], 10)
     hand_on(1)
     for cp in cps:
         cp.wait_recv()
@@ -435,12 +476,14 @@
 
 
 def finish(
-    full, pieces_ref, basis_moments_in, moments_in, basis_hbm, basis_moments_ref, moments_ref,
-    images, result, in_sem, out_sem, small_sem,
+    full, pieces_hbm, basis_moments_in, moments_in, basis_hbm, basis_moments_ref, moments_ref,
+    images, result, pieces_ref, in_sem, out_sem, small_sem,
 ):
     loads = [
         pltpu.make_async_copy(full.at[q], images.at[q], in_sem.at[q]) for q in range(PARTS)
     ]
+    get = pltpu.make_async_copy(pieces_hbm, pieces_ref, small_sem.at[2])
+    get.start()
     for cp in loads:
         cp.start()
     outs = [
@@ -449,6 +492,7 @@
     ]
     for cp in outs:
         cp.start()
+    get.wait()
     pieces = pieces_ref[...]
     for q in range(PARTS):
         loads[q].wait()
@@ -481,9 +525,14 @@
             jax.ShapeDtypeStruct((K, K), F32),
             jax.ShapeDtypeStruct((K, DESIGNS), F32),
         ),
-        in_specs=[any_spec, any_spec, vmem, vmem, vmem, vmem, pl.BlockSpec(memory_space=pltpu.SMEM)],
+        in_specs=[any_spec] * 7,
         out_specs=(any_spec, vmem, vmem, vmem),
         scratch_shapes=[
+            wide(K, K),
+            pltpu.VMEM((1, K), jnp.int32),
+            pltpu.VMEM((1, K), jnp.int32),
+            pltpu.VMEM((1, DESIGNS), jnp.int32),
+            wide(1, SLABS),
             low(PARTS, DESIGNS, ROWS, WIDE),
             *[low(ROWS, DESIGNS, WIDE)] * PARTS,
             low(ROWS, 2 * K, GIRTH),
@@ -495,10 +544,10 @@
             low(PARTS, 8, K, WIDE),
             low(PARTS, 8, K, WIDE),
             wide(PARTS, 8, K, WIDE),
-            low(PARTS, 8, K, WIDE),
-            low(PARTS, 3, 2, K, WIDE),
-            low(PARTS, 2, K, WIDE),
-            low(PARTS, 2, K, WIDE),
+            low(TRAVEL, 8, K, NARROW),
+            low(TRAVEL, 3, 2, K, NARROW),
+            low(TRAVEL, 2, K, NARROW),
+            low(TRAVEL, 2, K, NARROW),
             low(PARTS, 2, K, WIDE),
             wide(2, K // 2, 2 * K),
             wide(4, K // 2, 2 * K),
@@ -510,13 +559,14 @@
             dma((16,)), dma((16,)),
             dma((16,)), dma((16,)),
             dma((PARTS,)), dma((PARTS,)),
-            dma((PARTS, 3)), dma((PARTS, 3)),
-            dma((PARTS,)), dma((PARTS,)),
+            dma((TRAVEL, 3)), dma((TRAVEL, 3)),
+            dma((TRAVEL,)), dma((TRAVEL,)),
             dma((PARTS, 3)), dma((PARTS, 3)),
             dma((PARTS, 4)), dma((PARTS, 4)),
             dma((5,)), dma((5,)),
             dma((14,)), dma((14,)),
             dma((4,)),
+            dma((5,)),
         ],
         compiler_params=pltpu.CompilerParams(
             collective_id=0, has_side_effects=True, vmem_limit_bytes=60 << 20
@@ -524,7 +574,7 @@
     )(
         snapshots, start_basis, start_moments,
         station_power.reshape(1, K), girth_power.reshape(1, K),
-        slab_id.reshape(1, DESIGNS), slab_scale,
+        slab_id.reshape(1, DESIGNS), slab_scale.reshape(1, SLABS),
     )
     basis, basis_moments, moments = pl.pallas_call(
         finish,
@@ -533,12 +583,13 @@
             jax.ShapeDtypeStruct((K, K), F32),
             jax.ShapeDtypeStruct((K, DESIGNS), F32),
         ),
-        in_specs=[any_spec, vmem, any_spec, any_spec],
+        in_specs=[any_spec] * 4,
         out_specs=(any_spec, any_spec, any_spec),
         scratch_shapes=[
             low(PARTS, ROWS, K, WIDE),
             low(PARTS, ROWS, K, WIDE),
-            dma((PARTS,)), dma((PARTS,)), dma((2,)),
+            low(2 * K, K),
+            dma((PARTS,)), dma((PARTS,)), dma((3,)),
         ],
         compiler_params=pltpu.CompilerParams(vmem_limit_bytes=60 << 20),
     )(full, pieces, basis_moments, moments)

time: 77.9 us -> 75 us (0.963)
  Pallas kernels: 77 us -> 74.2 us
    pallas_call x1, Pallas kernels: 72.1 us -> 70 us  [body(): pl.pallas_call(kernel, out_shape=(jax.ShapeDtypeStruct((PARTS, ROWS, K, W...]
where the time goes in v3:
time: 75 us; the launch traced here: 74.8 us
  Pallas kernels  74.2 us (99%)
    pallas_call x1, Pallas kernels, body(): pl.pallas_call(kernel, out_shape=(jax.ShapeDtypeStruct((PARTS, ROWS, K, W...  70 us
    pallas_call x1, Pallas kernels, body(): pl.pallas_call(finish, out_shape=(jax.ShapeDtypeStruct((ROWS, K, GIRTH),...  4.19 us

profile of v3, /device:TPU:1, one launch (start us, length us, event | category | flops | bytes accessed | tf_op | source)
XLA Modules:
  0.0 74.8 jit_solution(4170654390441478410)
XLA Ops:
  0.6 70.0 %shard_map.94 = (bf16[4,16,64,256]{3,2,1,0:T(8,128)(2,1)}, bf16[128,64]{1,0:T(8,128)(2,1)}, f32[64,64]{1,0:T(8,128)}, f32[64,256]{1,0:T(8,128)}) custom-call(bf16[256,16,1024]{2,1,0:T(8,128)(2,1)} %snap_hbm.1, bf16[16,64,1024]{2,1,0:T(8,128)(2,1)} %start_hbm.1, f32[64,64]{1,0:T(8,128)} %moments_hbm.1, s32[1,64]{1,0:T(1,128)} %bitcast.6, s32[1,64]{1,0:T(1,128)} %bitcast.7, ...), custom_call_target="tpu_custom_call" | custom-call | tf_op jit(solution)/shard_map/pallas_call | solution.py:520
  70.7 4.2 %shard_map.95 = (bf16[16,64,1024]{2,1,0:T(8,128)(2,1)}, f32[64,64]{1,0:T(8,128)}, f32[64,256]{1,0:T(8,128)}) custom-call(bf16[4,16,64,256]{3,2,1,0:T(8,128)(2,1)} %get-tuple-element.10.full, bf16[128,64]{1,0:T(8,128)(2,1)} %get-tuple-element.11.pieces_hbm, f32[64,64]{1,0:T(8,128)} %get-tuple-element.12.basis_moments_in, f32[64,256]{1,0:T(8,128)} %get-tuple-element.13.moments_in), custom_call_target="tpu_custom_call" | custom-call | tf_op jit(solution)/shard_map/pallas_call | solution.py:579

commit v4 on v3

--- a/solution.py
+++ b/solution.py
@@ -53,7 +53,7 @@
             hooks[j]()
         b, r = j // 8, j % 8
         row = blocks[b][r : r + 1, :]
-        row = row / row[:, j : j + 1]
+        row = row * (1.0 / row[:, j : j + 1])
         for i in range(b, K // 8):
             col = blocks[i][:, j : j + 1]
             if i == b:
@@ -352,8 +352,8 @@
     def gather(q):
         pair = full.at[q, pl.ds(first, 2)]
         cps = [
-            send(image_ref.at[q], pair, g_s.at[q, r - 1], g_r.at[q, r - 1], along_y(r))
-            for r in (2, 1, 3)
+            send(image_ref.at[q], pair, g_s.at[q, r], g_r.at[q, r], along_y(2 * r + 1))
+            for r in range(2)
         ]
         send(image_ref.at[q], pair, f_s.at[q, 0], f_r.at[q, 0], sibling)
         own.append(pltpu.make_async_copy(image_ref.at[q], pair, own_sem.at[q]))
@@ -361,11 +361,23 @@
         return cps
 
     def hand_on(q):
-        for cp, r in zip(g_cp[q], (2, 1, 3)):
+        for cp, r in zip(g_cp[q], range(2)):
             cp.wait_recv()
-            frm = lax.rem(y + 4 - r, 4)
+            frm = lax.rem(y + 3 - 2 * r, 4)
+            station = full.at[q, pl.ds(c * 8 + 2 * frm + r, 1)]
+            relay[q].append(
+                send(station, station, g_s.at[q, 2 + r], g_r.at[q, 2 + r], along_y(2 * r + 1))
+            )
             pair = full.at[q, pl.ds(c * 8 + 2 * frm, 2)]
-            send(pair, pair, f_s.at[q, r], f_r.at[q, r], sibling)
+            send(pair, pair, f_s.at[q, 1 + r], f_r.at[q, 1 + r], sibling)
+
+    relay = [[] for q in range(PARTS)]
+
+    def hand_on_far(q):
+        for cp in relay[q]:
+            cp.wait_recv()
+        pair = full.at[q, pl.ds(c * 8 + 2 * lax.rem(y + 2, 4), 2)]
+        send(pair, pair, f_s.at[q, 3], f_r.at[q, 3], sibling)
 
     def exchange(ref, slot, members, sems):
         cps = []
@@ -413,7 +425,6 @@
     g_cp[0] = gather(0)
     for p in range(per, 2 * per):
         gram = settle(p, gram)
-    g_cp[1] = gather(1)
     im_cp.wait_recv()
     images_moments = unfold(im_z[0] + im_z[1])
     moments_part = lax.dot_general(
@@ -430,6 +441,7 @@
         to = at(zh, lax.rem(y + r // 2, 4), lax.rem(c + r % 2, 2))
         cps.append((r, to))
     cps = exchange(gram_1, me, cps, 0)
+    g_cp[1] = gather(1)
     g_cp[2] = gather(2)
     g_cp[3] = gather(3)
     for cp in cps:
@@ -445,11 +457,12 @@
     gram_3[zl] = (gram_2[0] + gram_2[1]) + (gram_2[2] + gram_2[3])
     cps = exchange(gram_3, zl, [(r, along_z(d)) for r, d in ((2, 2), (1, 1), (3, -1))], 10)
     hand_on(1)
+    hand_on_far(0)
     for cp in cps:
         cp.wait_recv()
     gram = unfold((gram_3[0] + gram_3[1]) + (gram_3[2] + gram_3[3])) + moments_part
     inverse = inverse_factor(
-        gram / (STATIONS * GIRTH), [(24, lambda: hand_on(2)), (48, lambda: hand_on(3))]
+        gram / (STATIONS * GIRTH), [(0, lambda: hand_on(2)), (16, lambda: hand_on(3)), (32, lambda: hand_on_far(1)), (40, lambda: hand_on_far(2)), (56, lambda: hand_on_far(3))]
     )
     basis_moments_out[...] = lax.dot_general(
         images_moments, inverse, (((1,), (1,)), ((), ())),
@@ -561,7 +574,7 @@
             dma((PARTS,)), dma((PARTS,)),
             dma((TRAVEL, 3)), dma((TRAVEL, 3)),
             dma((TRAVEL,)), dma((TRAVEL,)),
-            dma((PARTS, 3)), dma((PARTS, 3)),
+            dma((PARTS, 4)), dma((PARTS, 4)),
             dma((PARTS, 4)), dma((PARTS, 4)),
             dma((5,)), dma((5,)),
             dma((14,)), dma((14,)),

time: 75 us -> 75.5 us (level)
  no operation moved by 1% of the time
where the time goes in v4:
time: 75.5 us; the launch traced here: 75.4 us
  Pallas kernels  74.8 us (99%)
    pallas_call x1, Pallas kernels, body(): pl.pallas_call(kernel, out_shape=(jax.ShapeDtypeStruct((PARTS, ROWS, K, W...  70.6 us
    pallas_call x1, Pallas kernels, body(): pl.pallas_call(finish, out_shape=(jax.ShapeDtypeStruct((ROWS, K, GIRTH),...  4.19 us

profile of v4, /device:TPU:1, one launch (start us, length us, event | category | flops | bytes accessed | tf_op | source)
XLA Modules:
  0.0 75.4 jit_solution(8042921649465735455)
XLA Ops:
  0.6 70.6 %shard_map.94 = (bf16[4,16,64,256]{3,2,1,0:T(8,128)(2,1)}, bf16[128,64]{1,0:T(8,128)(2,1)}, f32[64,64]{1,0:T(8,128)}, f32[64,256]{1,0:T(8,128)}) custom-call(bf16[256,16,1024]{2,1,0:T(8,128)(2,1)} %snap_hbm.1, bf16[16,64,1024]{2,1,0:T(8,128)(2,1)} %start_hbm.1, f32[64,64]{1,0:T(8,128)} %moments_hbm.1, s32[1,64]{1,0:T(1,128)} %bitcast.6, s32[1,64]{1,0:T(1,128)} %bitcast.7, ...), custom_call_target="tpu_custom_call" | custom-call | tf_op jit(solution)/shard_map/pallas_call | solution.py:533
  71.2 4.2 %shard_map.95 = (bf16[16,64,1024]{2,1,0:T(8,128)(2,1)}, f32[64,64]{1,0:T(8,128)}, f32[64,256]{1,0:T(8,128)}) custom-call(bf16[4,16,64,256]{3,2,1,0:T(8,128)(2,1)} %get-tuple-element.10.full, bf16[128,64]{1,0:T(8,128)(2,1)} %get-tuple-element.11.pieces_hbm, f32[64,64]{1,0:T(8,128)} %get-tuple-element.12.basis_moments_in, f32[64,256]{1,0:T(8,128)} %get-tuple-element.13.moments_in), custom_call_target="tpu_custom_call" | custom-call | tf_op jit(solution)/shard_map/pallas_call | solution.py:592
